TPU v7x, 32 devices: a whole 2x2x4 slice. The times are simulated.
32 devices in a mesh: dp: 8 (over z, y), mp: 4 (over x, core).
Axes of the slice: x: 2, y: 2, z: 4, core: 2. Of those that a mesh axis runs over, the one named last changes fastest.
Arguments:
- stream_map: int32 [8], replicated, may hold values from 0 to 7, each once
- lengths: int32 [8], P('dp'), may hold values from 1 to 256, 1280 in all
- features: bfloat16 [8, 256, 2048], P('dp', None, 'mp'), may hold values from -6 to 6
- query_rows: bfloat16 [8, 256, 2048], P('dp', None, 'mp'), may hold values from -6 to 6
- key_rows: bfloat16 [8, 256, 2048], P('dp', None, 'mp'), may hold values from -6 to 6
- log_forget: float32 [8, 256, 4], P('dp', None, 'mp'), may hold values from -1 to 0, as said below
- in_gate: float32 [8, 256, 4], P('dp', None, 'mp'), may hold values from -2 to 2
- value_weight: bfloat16 [2048, 2048], P('dp', 'mp'), may hold values from -0.125 to 0.125
- state: float32 [8, 4, 512, 512], P('dp', 'mp'), may hold values from -0.5 to 0.5
- norm_state: float32 [8, 4, 512], P('dp', 'mp'), may hold values from -0.8 to 0.8
- cotangent: bfloat16 [8, 256, 2048], P('dp', None, 'mp'), may hold values from -6 to 6
Outputs:
- hidden: bfloat16 [8, 256, 2048], P('dp', None, 'mp')
- new_state: float32 [8, 4, 512, 512], P('dp', 'mp')
- new_norm: float32 [8, 4, 512], P('dp', 'mp')
- weight_grad: float32 [2048, 2048], P('dp', 'mp')
Inputs may be any that keep to these rules, and one draw needn't show every extreme that they name: stream_map is a permutation of the 8 slots. `lengths`: the largest length is exactly 256. `log_forget`: all entries negative.
All inputs are finite; a program needn't handle non-finite values. No bound on the sum of `lengths` on one device may be relied on, other than what follows from the above.
Results may differ from a plain program's by a relative error of at most 0.0065.
Values may be sent and summed in bfloat16 or wider, within the bound.
A program may use at most 64 MiB of HBM per device.

v0:
```python
import jax
import jax.numpy as jnp
from jax import lax
from jax.sharding import PartitionSpec as P


def migrate(stream_map, state, norm_state):
    slot_count = lax.axis_size("dp")
    head_width = state.shape[-1]
    row_part = head_width // slot_count
    blocks = state[0, 0].reshape(slot_count, row_part, head_width)
    norm_blocks = norm_state[0, 0].reshape(slot_count, row_part)
    spread, spread_norm = (
        lax.all_to_all(blocks, "dp", split_axis=0, concat_axis=0, tiled=True),
        lax.all_to_all(norm_blocks, "dp", split_axis=0, concat_axis=0, tiled=True),
    )
    source_slot = (
        jnp.zeros((slot_count,), jnp.int32)
        .at[stream_map]
        .set(jnp.arange(slot_count, dtype=jnp.int32))
    )
    picked = jnp.take(spread, source_slot, axis=0)
    picked_norm = jnp.take(spread_norm, source_slot, axis=0)
    returned, returned_norm = (
        lax.all_to_all(picked, "dp", split_axis=0, concat_axis=0, tiled=True),
        lax.all_to_all(picked_norm, "dp", split_axis=0, concat_axis=0, tiled=True),
    )
    return (returned.reshape(head_width, head_width), returned_norm.reshape(head_width))


def window_terms(feature_all, value_weight, queries, key_vectors, forget_logs, gate_logs, length):
    window = queries.shape[0]
    head_width = queries.shape[1]
    values = jnp.dot(
        feature_all,
        lax.all_gather(value_weight, "dp", axis=0, tiled=True),
        preferred_element_type=jnp.float32,
    ).astype(jnp.bfloat16)
    position = jnp.arange(window, dtype=jnp.int32)
    live_mask = (position < length).astype(jnp.float32)
    decays = jnp.cumsum(forget_logs * live_mask)
    weights_in = jnp.exp(gate_logs) * live_mask
    causal = position[:, None] >= position[None, :]
    gap_logs = jnp.where(causal, decays[:, None] - decays[None, :], -1e30)
    mixing = jnp.exp(gap_logs) * weights_in[None, :]
    scores = lax.dot_general(
        queries, key_vectors, (((1,), (1,)), ((), ())), preferred_element_type=jnp.float32
    ) * head_width ** (-0.5)
    combined = mixing * scores
    combined_low = combined.astype(jnp.bfloat16)
    local_numer = jnp.dot(combined_low, values, preferred_element_type=jnp.float32)
    local_inner = jnp.sum(combined, axis=1)
    return (values, live_mask, decays, weights_in, combined_low, local_numer, local_inner)


def on_device(
    stream_map,
    lengths,
    features,
    query_rows,
    key_rows,
    log_forget,
    in_gate,
    value_weight,
    state,
    norm_state,
    cotangent,
):
    feature_all = lax.all_gather(features, "mp", axis=2, tiled=True)[0]
    queries = query_rows[0]
    key_vectors = key_rows[0]
    head_width = queries.shape[1]
    window = queries.shape[0]
    start_state, start_norm = migrate(stream_map, state, norm_state)
    terms = window_terms(
        feature_all,
        value_weight,
        queries,
        key_vectors,
        log_forget[0, :, 0],
        in_gate[0, :, 0],
        lengths[0],
    )
    values, live_mask, decays, weights_in, combined_low, local_numer, local_inner = terms
    carried = jnp.exp(decays)
    query_wide = queries.astype(jnp.float32)
    from_state = jnp.dot(query_wide, start_state, precision=lax.Precision.HIGHEST)
    numer = carried[:, None] * from_state + local_numer
    inner_dot = (
        carried * jnp.dot(query_wide, start_norm, precision=lax.Precision.HIGHEST) + local_inner
    )
    denominator = jnp.maximum(jnp.abs(inner_dot), 1.0)
    hidden = (numer / denominator[:, None] * live_mask[:, None]).astype(jnp.bfloat16)
    final_decay = decays[window - 1]
    tail_weight = jnp.exp(final_decay - decays) * weights_in * head_width ** (-0.5)
    key_scaled = (key_vectors.astype(jnp.float32) * tail_weight[:, None]).astype(jnp.bfloat16)
    new_state = jnp.exp(final_decay) * start_state + lax.dot_general(
        key_scaled, values, (((0,), (0,)), ((), ())), preferred_element_type=jnp.float32
    )
    new_norm = jnp.exp(final_decay) * start_norm + jnp.dot(
        tail_weight, key_vectors.astype(jnp.float32), precision=lax.Precision.HIGHEST
    )
    scaled = (cotangent[0].astype(jnp.float32) * (live_mask / denominator)[:, None]).astype(
        jnp.bfloat16
    )
    value_grad = lax.dot_general(
        combined_low, scaled, (((0,), (0,)), ((), ())), preferred_element_type=jnp.float32
    ).astype(jnp.bfloat16)
    weight_grad = lax.psum_scatter(
        lax.dot_general(
            feature_all, value_grad, (((0,), (0,)), ((), ())), preferred_element_type=jnp.float32
        ),
        "dp",
        scatter_dimension=0,
        tiled=True,
    )
    return (hidden[None], new_state[None, None], new_norm[None, None], weight_grad)


def solution(mesh):
    return jax.shard_map(
        on_device,
        mesh=mesh,
        in_specs=(
            P(),
            P("dp"),
            P("dp", None, "mp"),
            P("dp", None, "mp"),
            P("dp", None, "mp"),
            P("dp", None, "mp"),
            P("dp", None, "mp"),
            P("dp", "mp"),
            P("dp", "mp", None, None),
            P("dp", "mp", None),
            P("dp", None, "mp"),
        ),
        out_specs=(
            P("dp", None, "mp"),
            P("dp", "mp", None, None),
            P("dp", "mp", None),
            P("dp", "mp"),
        ),
        check_vma=False,
    )
```

profile of v0, /device:TPU:10, one launch (start us, length us, event | category | flops | bytes accessed | tf_op | source)
XLA Modules:
  0.0 204.1 jit_solution(5070520903473724839)
XLA Ops:
  7.2 0.7 all-gather.3.cloned.1.call-update
  8.0 0.7 all-gather.5.cloned.1.call-update
  9.2 1.3 reduce.10
  10.5 0.7 all_to_all.20
  11.2 6.3 %all-to-all-start.2 = ((f32[8,1,64]{2,1,0:T(1,128)}), f32[8,1,64]{2,1,0:T(1,128)S(1)}, u32[]{:S(2)}, u32[]{:S(2)}) async-start(f32[8,1,64]{2,1,0:T(1,128)} %all_to_all.20), calls=%async_computation.2 | async-start | bytes 8192 | tf_op jit(solution)/shard_map/all_to_all | solution.py:15
  18.1 0.7 compare_select_fusion.3
  19.5 0.6 slice.12
  20.1 0.7 exp.56
  20.7 0.7 compare_select_fusion.1
  21.4 0.6 scatter_custom_fusion
  22.0 0.7 multiply_multiply_fusion
  22.7 0.6 gather_fusion.1
  23.3 0.7 bitcast_select_fusion
  23.9 6.0 %all-to-all-start.3 = ((f32[8,1,64]{2,1,0:T(1,128)}), f32[8,1,64]{2,1,0:T(1,128)S(1)}, u32[]{:S(2)}, u32[]{:S(2)}) async-start(f32[8,1,64]{2,1,0:T(1,128)} %bitcast.12), calls=%async_computation.3 | async-start | bytes 8192 | tf_op jit(solution)/shard_map/all_to_all | solution.py:26
  29.9 1.2 fusion.39
  31.2 3.7 %all-to-all-done.3 = f32[8,1,64]{2,1,0:T(1,128)S(1)} async-done(((f32[8,1,64]{2,1,0:T(1,128)}), f32[8,1,64]{2,1,0:T(1,128)S(1)}, u32[]{:S(2)}, u32[]{:S(2)}) %all-to-all-start.3) | async-done | bytes 2080 | tf_op jit(solution)/shard_map/all_to_all | solution.py:26
  34.8 0.7 reduce.11
  36.0 4.2 %convolution_bitcast_fusion = f32[2048,512]{0,1:T(8,128)} fusion(bf16[1,256,2048]{2,1,0:T(8,128)(2,1)} %all-gather.3.cloned.1.call-done, bf16[1,256,512]{2,1,0:T(8,128)(2,1)S(1)} %copy-done.4, f32[256]{0:T(256)S(1)} %get-tuple-element.16, bf16[256,256]{0,1:T(8,128)(2,1)S(1)} %get-tuple-element.23), kind=kOutput, calls=%fused_computation.3 | convolution fusion | flops 604504064 | bytes 5637120 | tf_op jit(solution)/shard_map/dot_general | solution.py:110
  40.2 1.2 copy-done.1
  41.4 44.3 %all_to_all.28 = f32[8,64,512]{2,1,0:T(8,128)S(1)} all-to-all(f32[8,64,512]{2,1,0:T(8,128)S(1)} %bitcast.86), channel_id=1, replica_groups=mesh['dp'=8,'mp'=4] {'dp'}, dimensions={0} | all-to-all | bytes 2097152 | tf_op jit(solution)/shard_map/all_to_all | solution.py:14
  85.7 0.6 gather_fusion
  86.3 1.2 broadcast_select_fusion
  87.5 6.0 %all-to-all-start.1 = ((f32[8,64,512]{2,1,0:T(8,128)}), f32[8,64,512]{2,1,0:T(8,128)S(1)}, u32[]{:S(2)}, u32[]{:S(2)}) async-start(f32[8,64,512]{2,1,0:T(8,128)} %broadcast_select_fusion), calls=%async_computation.1 | async-start | bytes 2097152 | tf_op jit(solution)/shard_map/all_to_all | solution.py:25
  94.3 0.7 fusion.31
  95.3 0.6 multiply_add_fusion
  95.9 2.3 %convolution_convert_fusion.1 = bf16[256,512]{1,0:T(8,128)(2,1)S(1)} fusion(bf16[2048,512]{1,0:T(8,128)(2,1)} %all-gather.5.cloned.1.call-done, bf16[1,256,2048]{2,1,0:T(8,128)(2,1)S(1)} %copy-done.2), kind=kOutput, calls=%fused_computation.13 | convolution fusion | flops 537001984 | bytes 3407872 | tf_op jit(solution)/shard_map/dot_general | solution.py:34
  98.5 32.0 %all-to-all-done.1 = f32[8,64,512]{2,1,0:T(8,128)S(1)} async-done(((f32[8,64,512]{2,1,0:T(8,128)}), f32[8,64,512]{2,1,0:T(8,128)S(1)}, u32[]{:S(2)}, u32[]{:S(2)}) %all-to-all-start.1) | async-done | bytes 1048608 | tf_op jit(solution)/shard_map/all_to_all | solution.py:25
  130.4 1.0 fusion.7
  131.4 0.8 copy.23
  132.3 1.4 fusion
  133.7 61.9 %reduce-scatter.2.cloned.1.call-done = f32[256,512]{0,1:T(8,128)} async-done(((f32[2048,512]{0,1:T(8,128)}), f32[256,512]{0,1:T(8,128)}) %reduce-scatter.2.cloned.1.call-update) | async-done | bytes 524304 | tf_op jit(solution)/shard_map/reduce_scatter | solution.py:109
  195.6 2.0 copy.24
  (34 shorter events, 2.3 us)
Async XLA Ops:
  7.2 22.8 %copy-start = (bf16[1,256,512]{2,1,0:T(8,128)(2,1)S(1)}, bf16[1,256,512]{2,1,0:T(8,128)(2,1)}, u32[]{:S(2)}) copy-start(bf16[1,256,512]{2,1,0:T(8,128)(2,1)} %param.14) | copy-start | bytes 786436
  7.2 28.8 %copy-start.4 = (bf16[1,256,512]{2,1,0:T(8,128)(2,1)S(1)}, bf16[1,256,512]{2,1,0:T(8,128)(2,1)}, u32[]{:S(2)}) copy-start(bf16[1,256,512]{2,1,0:T(8,128)(2,1)} %param.21) | copy-start | bytes 786436
  7.2 28.7 %all-gather.3.cloned.1.call-start = ((), (), s32[]{:S(2)}) async-start(), calls=%async_computation.5 | async-start | bytes 1310720 | tf_op jit(solution)/shard_map/all_gather | solution.py:69
  7.9 88.0 %all-gather.5.cloned.1.call-start = ((), (), s32[]{:S(2)}) async-start(), calls=%async_computation.6 | async-start | bytes 2359296 | tf_op jit(solution)/shard_map/all_gather | solution.py:36
  11.2 11.5 %all-to-all-start.2 = ((f32[8,1,64]{2,1,0:T(1,128)}), f32[8,1,64]{2,1,0:T(1,128)S(1)}, u32[]{:S(2)}, u32[]{:S(2)}) async-start(f32[8,1,64]{2,1,0:T(1,128)} %all_to_all.20), calls=%async_computation.2 | async-start | bytes 8192 | tf_op jit(solution)/shard_map/all_to_all | solution.py:15
  23.9 10.9 %all-to-all-start.3 = ((f32[8,1,64]{2,1,0:T(1,128)}), f32[8,1,64]{2,1,0:T(1,128)S(1)}, u32[]{:S(2)}, u32[]{:S(2)}) async-start(f32[8,1,64]{2,1,0:T(1,128)} %bitcast.12), calls=%async_computation.3 | async-start | bytes 8192 | tf_op jit(solution)/shard_map/all_to_all | solution.py:26
  29.9 165.6 %reduce-scatter.2.cloned.1.call-start = ((), (), s32[]{:S(2)}) async-start(), calls=%async_computation.7 | async-start | bytes 4718592 | tf_op jit(solution)/shard_map/reduce_scatter | solution.py:109
  40.2 1.2 copy-start.1
  86.3 8.7 %copy-start.3 = (bf16[1,256,512]{2,1,0:T(8,128)(2,1)S(1)}, bf16[1,256,512]{2,1,0:T(8,128)(2,1)}, u32[]{:S(2)}) copy-start(bf16[1,256,512]{2,1,0:T(8,128)(2,1)} %param.15) | copy-start | bytes 786436
  86.3 9.6 %copy-start.2 = (bf16[1,256,2048]{2,1,0:T(8,128)(2,1)S(1)}, bf16[1,256,2048]{2,1,0:T(8,128)(2,1)}, u32[]{:S(2)}) copy-start(bf16[1,256,2048]{2,1,0:T(8,128)(2,1)} %all-gather.3.cloned.1.call-done) | copy-start | bytes 3145732
  87.5 42.9 %all-to-all-start.1 = ((f32[8,64,512]{2,1,0:T(8,128)}), f32[8,64,512]{2,1,0:T(8,128)S(1)}, u32[]{:S(2)}, u32[]{:S(2)}) async-start(f32[8,64,512]{2,1,0:T(8,128)} %broadcast_select_fusion), calls=%async_computation.1 | async-start | bytes 2097152 | tf_op jit(solution)/shard_map/all_to_all | solution.py:25
Sparse Core Ops, SparseCore 0:
  9.6 16.9 all-gather.2
  28.7 61.4 all-gather.4
  93.8 101.6 reduce-scatter.1
where the time goes:
time: 206 us; the launch traced here: 204 us
  waiting for transfers between devices  98.9 us (48%)
  blocking collectives  44.3 us (22%)
  starting transfers between devices  18.4 us (9%)
  between operations  15.3 us (7%)
  matrix products  10.9 us (5%)
  local copies, waits for them, and re-layouts  8.68 us (4%)
  other arithmetic  7.68 us (4%)
    reduce_scatter x1, waiting for transfers between devices, on_device(): lax.psum_scatter(lax.dot_general(feature_all, value_grad, (((0,), (0,)),...  61.9 us
    all_to_all x1, blocking collectives, migrate(): lax.all_to_all(blocks, 'dp', split_axis=0, concat_axis=0, tiled=True)  44.3 us
    all_to_all x1, waiting for transfers between devices, migrate(): lax.all_to_all(picked, 'dp', split_axis=0, concat_axis=0, tiled=True)  32 us
    all_to_all x1, starting transfers between devices, migrate(): lax.all_to_all(norm_blocks, 'dp', split_axis=0, concat_axis=0, tiled=True)  6.28 us
    all_to_all x1, starting transfers between devices, migrate(): lax.all_to_all(picked, 'dp', split_axis=0, concat_axis=0, tiled=True)  6.04 us
    all_to_all x1, starting transfers between devices, migrate(): lax.all_to_all(picked_norm, 'dp', split_axis=0, concat_axis=0, tiled=True)  5.99 us
    unnamed x13, local copies, waits for them, and re-layouts  4.62 us
    dot_general x1, matrix products, on_device(): lax.dot_general(feature_all, value_grad, (((0,), (0,)), ((), ())), prefer...  4.22 us
  transfers between devices with their start and end apart: 6, of which 3 were waited for; matrix products, arithmetic and copies ran while one was open for 11% of the time, Pallas kernels for 0%

commit v1 on v0

--- a/solution.py
+++ b/solution.py
@@ -8,24 +8,20 @@
     slot_count = lax.axis_size("dp")
     head_width = state.shape[-1]
     row_part = head_width // slot_count
-    blocks = state[0, 0].reshape(slot_count, row_part, head_width)
-    norm_blocks = norm_state[0, 0].reshape(slot_count, row_part)
-    spread, spread_norm = (
-        lax.all_to_all(blocks, "dp", split_axis=0, concat_axis=0, tiled=True),
-        lax.all_to_all(norm_blocks, "dp", split_axis=0, concat_axis=0, tiled=True),
-    )
-    source_slot = (
-        jnp.zeros((slot_count,), jnp.int32)
-        .at[stream_map]
-        .set(jnp.arange(slot_count, dtype=jnp.int32))
-    )
-    picked = jnp.take(spread, source_slot, axis=0)
-    picked_norm = jnp.take(spread_norm, source_slot, axis=0)
-    returned, returned_norm = (
-        lax.all_to_all(picked, "dp", split_axis=0, concat_axis=0, tiled=True),
-        lax.all_to_all(picked_norm, "dp", split_axis=0, concat_axis=0, tiled=True),
-    )
-    return (returned.reshape(head_width, head_width), returned_norm.reshape(head_width))
+    blocks = state[0, 0].astype(jnp.bfloat16).reshape(slot_count, row_part, head_width)
+    spread = lax.all_to_all(blocks, "dp", split_axis=0, concat_axis=0, tiled=True)
+    norms = lax.all_gather(norm_state[0, 0], "dp", axis=0, tiled=False)
+    chosen = jnp.arange(slot_count, dtype=jnp.int32)[:, None] == stream_map[None, :]
+    picked = jnp.einsum(
+        "ps,src->prc",
+        chosen.astype(jnp.bfloat16),
+        spread,
+        preferred_element_type=jnp.float32,
+    ).astype(jnp.bfloat16)
+    returned = lax.all_to_all(picked, "dp", split_axis=0, concat_axis=0, tiled=True)
+    mine = lax.axis_index("dp") == stream_map
+    start_norm = jnp.sum(jnp.where(mine[:, None], norms, 0.0), axis=0)
+    return (returned.reshape(head_width, head_width), start_norm)
 
 
 def window_terms(feature_all, value_weight, queries, key_vectors, forget_logs, gate_logs, length):
@@ -38,9 +34,9 @@
     ).astype(jnp.bfloat16)
     position = jnp.arange(window, dtype=jnp.int32)
     live_mask = (position < length).astype(jnp.float32)
-    decays = jnp.cumsum(forget_logs * live_mask)
     weights_in = jnp.exp(gate_logs) * live_mask
     causal = position[:, None] >= position[None, :]
+    decays = jnp.sum(jnp.where(causal, (forget_logs * live_mask)[None, :], 0.0), axis=1)
     gap_logs = jnp.where(causal, decays[:, None] - decays[None, :], -1e30)
     mixing = jnp.exp(gap_logs) * weights_in[None, :]
     scores = lax.dot_general(
@@ -84,21 +80,21 @@
     values, live_mask, decays, weights_in, combined_low, local_numer, local_inner = terms
     carried = jnp.exp(decays)
     query_wide = queries.astype(jnp.float32)
-    from_state = jnp.dot(query_wide, start_state, precision=lax.Precision.HIGHEST)
+    from_state = jnp.dot(queries, start_state, preferred_element_type=jnp.float32)
     numer = carried[:, None] * from_state + local_numer
     inner_dot = (
-        carried * jnp.dot(query_wide, start_norm, precision=lax.Precision.HIGHEST) + local_inner
+        carried * jnp.sum(query_wide * start_norm[None, :], axis=1) + local_inner
     )
     denominator = jnp.maximum(jnp.abs(inner_dot), 1.0)
     hidden = (numer / denominator[:, None] * live_mask[:, None]).astype(jnp.bfloat16)
     final_decay = decays[window - 1]
     tail_weight = jnp.exp(final_decay - decays) * weights_in * head_width ** (-0.5)
     key_scaled = (key_vectors.astype(jnp.float32) * tail_weight[:, None]).astype(jnp.bfloat16)
-    new_state = jnp.exp(final_decay) * start_state + lax.dot_general(
+    new_state = jnp.exp(final_decay) * start_state.astype(jnp.float32) + lax.dot_general(
         key_scaled, values, (((0,), (0,)), ((), ())), preferred_element_type=jnp.float32
     )
-    new_norm = jnp.exp(final_decay) * start_norm + jnp.dot(
-        tail_weight, key_vectors.astype(jnp.float32), precision=lax.Precision.HIGHEST
+    new_norm = jnp.exp(final_decay) * start_norm + jnp.sum(
+        tail_weight[:, None] * key_vectors.astype(jnp.float32), axis=0
     )
     scaled = (cotangent[0].astype(jnp.float32) * (live_mask / denominator)[:, None]).astype(
         jnp.bfloat16

time: 206 us -> 191 us (0.927)
  starting transfers between devices: 18.4 us -> 7.52 us
  other arithmetic: 7.68 us -> 4.1 us
  blocking collectives: 44.3 us -> 47.8 us
  local copies, waits for them, and re-layouts: 8.68 us -> 6.33 us
    all_gather x0 -> x1, blocking collectives: none -> 25.1 us  [migrate(): norms = lax.all_gather(norm_state[0, 0], 'dp', axis=0, tiled=False)]
    reduce_scatter x1, waiting for transfers between devices: 61.9 us -> 85.4 us  [on_device(): lax.psum_scatter(lax.dot_general(feature_all, value_grad, (((0,), (0,)),...]
    all_to_all x1, blocking collectives: 44.3 us -> 22.6 us  [migrate(): lax.all_to_all(blocks, 'dp', split_axis=0, concat_axis=0, tiled=True)]
    all_to_all x1, waiting for transfers between devices: 32 us -> 10.8 us  [migrate(): lax.all_to_all(picked, 'dp', split_axis=0, concat_axis=0, tiled=True)]
    all_to_all x2 -> x0, starting transfers between devices: 12.3 us -> none  [the longest x1 6.28 us: migrate(): lax.all_to_all(norm_blocks, 'dp', split_axis=0, concat_axis=0, tiled=True)]
    all_to_all x2 -> x0, waiting for transfers between devices: 3.66 us -> none  [the longest x1 3.66 us: migrate(): lax.all_to_all(picked_norm, 'dp', split_axis=0, concat_axis=0, tiled=True)]
    select_n x4 -> x0, other arithmetic: 2.52 us -> none  [the longest x2 1.19 us: migrate(): picked = jnp.take(spread, source_slot, axis=0)]
    unnamed x13 -> x14, local copies, waits for them, and re-layouts: 4.62 us -> 4.1 us
  transfers between devices with their start and end apart: 6 -> 4, of which waited for: 3 -> 2; matrix products, arithmetic and copies ran while one was open for 11% -> 9% of each run, Pallas kernels for 0% -> 0%
where the time goes in v1:
time: 191 us; the launch traced here: 189 us
  waiting for transfers between devices  97.7 us (51%)
  blocking collectives  47.8 us (25%)
  between operations  15.2 us (8%)
  matrix products  10.2 us (5%)
  starting transfers between devices  7.52 us (4%)
  local copies, waits for them, and re-layouts  6.33 us (3%)
  other arithmetic  4.1 us (2%)
    reduce_scatter x1, waiting for transfers between devices, on_device(): lax.psum_scatter(lax.dot_general(feature_all, value_grad, (((0,), (0,)),...  85.4 us
    all_gather x1, blocking collectives, migrate(): norms = lax.all_gather(norm_state[0, 0], 'dp', axis=0, tiled=False)  25.1 us
    all_to_all x1, blocking collectives, migrate(): lax.all_to_all(blocks, 'dp', split_axis=0, concat_axis=0, tiled=True)  22.6 us
    all_to_all x1, waiting for transfers between devices, migrate(): lax.all_to_all(picked, 'dp', split_axis=0, concat_axis=0, tiled=True)  10.8 us
    all_to_all x1, starting transfers between devices, migrate(): lax.all_to_all(picked, 'dp', split_axis=0, concat_axis=0, tiled=True)  7.41 us
    dot_general x1, matrix products, on_device(): lax.dot_general(feature_all, value_grad, (((0,), (0,)), ((), ())), prefer...  4.19 us
    unnamed x14, local copies, waits for them, and re-layouts  4.1 us
  transfers between devices with their start and end apart: 4, of which 2 were waited for; matrix products, arithmetic and copies ran while one was open for 9% of the time, Pallas kernels for 0%

profile of v1, /device:TPU:10, one launch (start us, length us, event | category | flops | bytes accessed | tf_op | source)
XLA Modules:
  0.0 188.8 jit_solution(2201307896623173694)
XLA Ops:
  7.2 0.0 all-gather.4.cloned.1.call-start
  7.2 0.7 all-gather.4.cloned.1.call-update
  7.9 0.0 all-gather.6.cloned.1.call-start
  8.0 0.7 all-gather.6.cloned.1.call-update
  8.7 0.0 reduce-scatter.2.cloned.1.call-start
  9.4 0.7 fusion.34
  10.0 0.1 select_reduce_fusion
  10.2 0.6 slice.3
  10.7 0.7 exp.43
  11.4 25.1 %all-gather = f32[8,1,512]{2,1,0:T(1,128)S(1)} all-gather(f32[1,1,512]{2,1,0:T(1,128)} %param.20), channel_id=2, replica_groups=mesh['dp'=8,'mp'=4] {'dp'}, dimensions={0}, use_global_device_ids=true | all-gather | bytes 18432 | tf_op jit(solution)/shard_map/all_gather | solution.py:13
  36.6 0.7 broadcast_compare_fusion
  37.2 0.1 fusion.28
  37.3 1.1 multiply_reduce_fusion
  38.4 0.7 multiply_multiply_fusion
  39.1 1.3 fusion.37
  40.4 4.2 %convolution_bitcast_fusion = f32[2048,512]{0,1:T(8,128)} fusion(bf16[1,256,2048]{2,1,0:T(8,128)(2,1)} %all-gather.4.cloned.1.call-done, bf16[1,256,512]{2,1,0:T(8,128)(2,1)S(1)} %copy-done.4, f32[256]{0:T(256)S(1)} %get-tuple-element.16, bf16[256,256]{0,1:T(8,128)(2,1)S(1)} %get-tuple-element.22), kind=kOutput, calls=%fused_computation | convolution fusion | flops 604504064 | bytes 5637120 | tf_op jit(solution)/shard_map/dot_general | solution.py:106
  44.6 1.2 copy-done.1
  45.9 0.1 convert_element_type.55
  45.9 22.6 %all_to_all.10 = bf16[8,64,512]{2,1,0:T(8,128)(2,1)S(1)} all-to-all(bf16[8,64,512]{2,1,0:T(8,128)(2,1)S(1)} %bitcast.64), channel_id=1, replica_groups=mesh['dp'=8,'mp'=4] {'dp'}, dimensions={0} | all-to-all | bytes 1048576 | tf_op jit(solution)/shard_map/all_to_all | solution.py:12
  68.6 0.4 convolution_convert_fusion
  69.0 0.9 copy.24
  69.9 7.4 %all-to-all-start.1 = ((bf16[8,64,512]{2,1,0:T(8,128)(2,1)}), bf16[8,64,512]{2,1,0:T(8,128)(2,1)S(1)}, u32[]{:S(2)}, u32[]{:S(2)}) async-start(bf16[8,64,512]{2,1,0:T(8,128)(2,1)} %copy.24), calls=%async_computation.1 | async-start | bytes 1048576 | tf_op jit(solution)/shard_map/all_to_all | solution.py:21
  78.1 0.1 fusion.11
  78.2 0.6 multiply_add_fusion
  78.8 10.8 %all-to-all-done.1 = bf16[8,64,512]{2,1,0:T(8,128)(2,1)S(1)} async-done(((bf16[8,64,512]{2,1,0:T(8,128)(2,1)}), bf16[8,64,512]{2,1,0:T(8,128)(2,1)S(1)}, u32[]{:S(2)}, u32[]{:S(2)}) %all-to-all-start.1) | async-done | bytes 524320 | tf_op jit(solution)/shard_map/all_to_all | solution.py:21
  89.6 0.3 fusion.3
  90.0 2.3 %convolution_convert_fusion.2 = bf16[256,512]{1,0:T(8,128)(2,1)S(1)} fusion(bf16[2048,512]{1,0:T(8,128)(2,1)} %all-gather.6.cloned.1.call-done, bf16[1,256,2048]{2,1,0:T(8,128)(2,1)S(1)} %copy-done.3), kind=kOutput, calls=%fused_computation.11 | convolution fusion | flops 537001984 | bytes 3407872 | tf_op jit(solution)/shard_map/dot_general | solution.py:30
  92.3 0.3 fusion.6
  92.6 0.8 copy.26
  93.4 1.4 fusion
  94.8 85.4 %reduce-scatter.2.cloned.1.call-done = f32[256,512]{0,1:T(8,128)} async-done(((f32[2048,512]{0,1:T(8,128)}), f32[256,512]{0,1:T(8,128)}) %reduce-scatter.2.cloned.1.call-update) | async-done | bytes 524304 | tf_op jit(solution)/shard_map/reduce_scatter | solution.py:105
  180.3 2.0 %copy.27 = f32[256,512]{1,0:T(8,128)} copy(f32[256,512]{0,1:T(8,128)} %reduce-scatter.2.cloned.1.call-done) | data formatting | bytes 1048576
  (16 shorter events, 0.1 us)
Async XLA Ops:
  7.2 33.3 %copy-start.4 = (bf16[1,256,512]{2,1,0:T(8,128)(2,1)S(1)}, bf16[1,256,512]{2,1,0:T(8,128)(2,1)}, u32[]{:S(2)}) copy-start(bf16[1,256,512]{2,1,0:T(8,128)(2,1)} %param.21) | copy-start | bytes 786436
  7.2 33.2 %all-gather.4.cloned.1.call-start = ((), (), s32[]{:S(2)}) async-start(), calls=%async_computation.3 | async-start | bytes 1310720 | tf_op jit(solution)/shard_map/all_gather | solution.py:65
  7.9 82.1 %all-gather.6.cloned.1.call-start = ((), (), s32[]{:S(2)}) async-start(), calls=%async_computation.4 | async-start | bytes 2359296 | tf_op jit(solution)/shard_map/all_gather | solution.py:32
  8.7 171.6 %reduce-scatter.2.cloned.1.call-start = ((), (), s32[]{:S(2)}) async-start(), calls=%async_computation.5 | async-start | bytes 4718592 | tf_op jit(solution)/shard_map/reduce_scatter | solution.py:105
  44.6 1.2 copy-start.1
  45.8 22.7 %copy-start.5 = (s32[8]{0:T(128)S(1)}, s32[8]{0:T(128)}, u32[]{:S(2)}) copy-start(s32[8]{0:T(128)} %param.11) | copy-start | bytes 100
  45.9 32.1 %copy-start = (bf16[1,256,512]{2,1,0:T(8,128)(2,1)S(1)}, bf16[1,256,512]{2,1,0:T(8,128)(2,1)}, u32[]{:S(2)}) copy-start(bf16[1,256,512]{2,1,0:T(8,128)(2,1)} %param.15) | copy-start | bytes 786436
  45.9 43.7 %copy-start.2 = (bf16[1,256,512]{2,1,0:T(8,128)(2,1)S(1)}, bf16[1,256,512]{2,1,0:T(8,128)(2,1)}, u32[]{:S(2)}) copy-start(bf16[1,256,512]{2,1,0:T(8,128)(2,1)} %param.14) | copy-start | bytes 786436
  69.0 21.0 %copy-start.3 = (bf16[1,256,2048]{2,1,0:T(8,128)(2,1)S(1)}, bf16[1,256,2048]{2,1,0:T(8,128)(2,1)}, u32[]{:S(2)}) copy-start(bf16[1,256,2048]{2,1,0:T(8,128)(2,1)} %all-gather.4.cloned.1.call-done) | copy-start | bytes 3145732
  69.9 19.7 %all-to-all-start.1 = ((bf16[8,64,512]{2,1,0:T(8,128)(2,1)}), bf16[8,64,512]{2,1,0:T(8,128)(2,1)S(1)}, u32[]{:S(2)}, u32[]{:S(2)}) async-start(bf16[8,64,512]{2,1,0:T(8,128)(2,1)} %copy.24), calls=%async_computation.1 | async-start | bytes 1048576 | tf_op jit(solution)/shard_map/all_to_all | solution.py:21
Sparse Core Ops, SparseCore 0:
  9.6 16.9 all-gather.3
  28.7 57.2 all-gather.5
  89.6 90.6 reduce-scatter.1

commit v2 on v1

--- a/solution.py
+++ b/solution.py
@@ -1,6 +1,10 @@
+import functools
+
 import jax
 import jax.numpy as jnp
 from jax import lax
+from jax.experimental import pallas as pl
+from jax.experimental.pallas import tpu as pltpu
 from jax.sharding import PartitionSpec as P
 
 
@@ -49,7 +53,7 @@
     return (values, live_mask, decays, weights_in, combined_low, local_numer, local_inner)
 
 
-def on_device(
+def with_collectives(
     stream_map,
     lengths,
     features,
@@ -113,6 +117,351 @@
     return (hidden[None], new_state[None, None], new_norm[None, None], weight_grad)
 
 
+def remote(src, dst, send_sem, recv_sem, peer):
+    return pltpu.make_async_remote_copy(
+        src_ref=src,
+        dst_ref=dst,
+        send_sem=send_sem,
+        recv_sem=recv_sem,
+        device_id=peer,
+        device_id_type=pl.DeviceIdType.MESH,
+    )
+
+
+def window_kernel(
+    slots,
+    heads,
+    map_ref,
+    length_ref,
+    f_ref,
+    q_ref,
+    k_ref,
+    forget_ref,
+    gate_ref,
+    w_ref,
+    s_ref,
+    n_ref,
+    cot_ref,
+    hidden_ref,
+    state_ref,
+    norm_ref,
+    grad_ref,
+    fbuf,
+    wbuf,
+    nbuf,
+    sblk,
+    s1,
+    picked,
+    s2,
+    part,
+    psend,
+    yrecv,
+    zsend,
+    zrecv,
+    f_sems,
+    n_sems,
+    s1_sems,
+    s2_sems,
+    wz_sems,
+    wy_sems,
+    y_sems,
+    z_sems,
+):
+    lines = slots // 2
+    me = lax.axis_index("dp")
+    head = lax.axis_index("mp")
+    z, y = me // 2, lax.rem(me, 2)
+    other = 1 - y
+    pair = {"dp": z * 2 + other}
+
+    def ahead(k):
+        return lax.rem(me + k, slots)
+
+    def line_ahead(k):
+        return lax.rem(z + k, lines)
+
+    barrier = pltpu.get_barrier_semaphore()
+    for k in range(1, slots):
+        pl.semaphore_signal(
+            barrier, inc=1, device_id={"dp": ahead(k)}, device_id_type=pl.DeviceIdType.MESH
+        )
+    for k in range(1, heads):
+        pl.semaphore_signal(
+            barrier,
+            inc=1,
+            device_id={"mp": lax.rem(head + k, heads)},
+            device_id_type=pl.DeviceIdType.MESH,
+        )
+    pl.semaphore_wait(barrier, slots + heads - 2)
+
+    norm_copies = [
+        remote(n_ref, nbuf.at[me], n_sems.at[0, k], n_sems.at[1, k], {"dp": ahead(k)})
+        for k in range(1, slots)
+    ]
+    feature_copies = [
+        remote(
+            f_ref,
+            fbuf.at[head],
+            f_sems.at[0, k],
+            f_sems.at[1, k],
+            {"mp": lax.rem(head + k, heads)},
+        )
+        for k in range(1, heads)
+    ]
+    for copy in norm_copies + feature_copies:
+        copy.start()
+    sblk[...] = s_ref[...].astype(jnp.bfloat16)
+    spread_copies = [
+        remote(
+            sblk.at[ahead(k)], s1.at[me], s1_sems.at[0, k], s1_sems.at[1, k], {"dp": ahead(k)}
+        )
+        for k in range(1, slots)
+    ]
+    for copy in spread_copies:
+        copy.start()
+    line_copies = [
+        remote(
+            w_ref,
+            wbuf.at[me],
+            wz_sems.at[0, k],
+            wz_sems.at[1, k],
+            {"dp": line_ahead(k) * 2 + y},
+        )
+        for k in range(1, lines)
+    ]
+    pair_copies = [remote(w_ref, wbuf.at[me], wy_sems.at[0, 0], wy_sems.at[1, 0], pair)]
+    pair_copies[0].start()
+    for copy in line_copies:
+        copy.start()
+
+    nbuf[me] = n_ref[...]
+    fbuf[head] = f_ref[...]
+    wbuf[me] = w_ref[...]
+    s1[me] = sblk[me]
+
+    window, width = q_ref.shape
+    length = length_ref[0]
+    row = lax.broadcasted_iota(jnp.int32, (window, window), 0)
+    column = lax.broadcasted_iota(jnp.int32, (window, window), 1)
+    causal = row >= column
+    diagonal = row == column
+    live = (lax.broadcasted_iota(jnp.int32, (window, 1), 0) < length).astype(jnp.float32)
+
+    def as_row(x):
+        return jnp.sum(jnp.where(diagonal, x, 0.0), axis=0, keepdims=True)
+
+    weights_in = jnp.exp(gate_ref[...]) * live
+    decays = jnp.sum(
+        jnp.where(causal, as_row(forget_ref[...] * live), 0.0), axis=1, keepdims=True
+    )
+    mixing = jnp.exp(jnp.where(causal, decays - as_row(decays), -1e30)) * as_row(weights_in)
+    scale = width**-0.5
+    scores = lax.dot_general(
+        q_ref[...], k_ref[...], (((1,), (1,)), ((), ())), preferred_element_type=jnp.float32
+    )
+    combined = mixing * (scores * scale)
+    combined_low = combined.astype(jnp.bfloat16)
+    carried = jnp.exp(decays)
+    final_decay = decays[window - 1 : window, :]
+    kept = jnp.exp(final_decay)
+    tail = jnp.exp(final_decay - decays) * weights_in * scale
+    key_wide = k_ref[...].astype(jnp.float32) * tail
+    key_scaled = key_wide.astype(jnp.bfloat16)
+
+    def source_of(p):
+        found = jnp.int32(0)
+        for s in range(slots):
+            found = jnp.where(map_ref[s] == p, jnp.int32(s), found)
+        return found
+
+    for copy in norm_copies:
+        copy.wait()
+    start_norm = nbuf[source_of(me)]
+    norm_ref[...] = kept * start_norm + jnp.sum(key_wide, axis=0, keepdims=True)
+    inner = carried * jnp.sum(
+        q_ref[...].astype(jnp.float32) * start_norm, axis=1, keepdims=True
+    ) + jnp.sum(combined, axis=1, keepdims=True)
+    denominator = jnp.maximum(jnp.abs(inner), 1.0)
+    scaled = (cot_ref[...].astype(jnp.float32) * (live / denominator)).astype(jnp.bfloat16)
+    value_grad = lax.dot_general(
+        combined_low, scaled, (((0,), (0,)), ((), ())), preferred_element_type=jnp.float32
+    ).astype(jnp.bfloat16)
+
+    for copy in spread_copies:
+        copy.wait()
+    for p in range(slots):
+        picked[p] = s1[source_of(p)]
+    return_copies = [
+        remote(
+            picked.at[ahead(k)], s2.at[me], s2_sems.at[0, k], s2_sems.at[1, k], {"dp": ahead(k)}
+        )
+        for k in range(1, slots)
+    ]
+    for copy in return_copies:
+        copy.start()
+    s2[me] = picked[me]
+
+    for copy in feature_copies:
+        copy.wait()
+    rows = grad_ref.shape[0]
+    per_head = f_ref.shape[1] // rows
+    for r in range(slots):
+        lower = (r % per_head) * rows
+        block = lax.dot_general(
+            fbuf[r // per_head, :, lower : lower + rows],
+            value_grad,
+            (((0,), (0,)), ((), ())),
+            preferred_element_type=jnp.float32,
+        )
+        part[r] = block
+        psend[r] = block.astype(jnp.bfloat16)
+    order = list(range(1, lines)) + [0]
+    y_copies = [
+        remote(
+            psend.at[line_ahead(k) * 2 + other],
+            yrecv.at[line_ahead(k)],
+            y_sems.at[0, k],
+            y_sems.at[1, k],
+            pair,
+        )
+        for k in order
+    ]
+    for copy in y_copies:
+        copy.start()
+
+    for k in range(1, lines):
+        line_copies[k - 1].wait()
+        slot = lax.rem(z + lines - k, lines) * 2 + y
+        forward = remote(wbuf.at[slot], wbuf.at[slot], wy_sems.at[0, k], wy_sems.at[1, k], pair)
+        forward.start()
+        pair_copies.append(forward)
+
+    z_copies = []
+    for k, copy in zip(order, y_copies):
+        copy.wait()
+        if k == 0:
+            continue
+        to = line_ahead(k)
+        zsend[to] = (part[to * 2 + y] + yrecv[to].astype(jnp.float32)).astype(jnp.bfloat16)
+        out = remote(
+            zsend.at[to], zrecv.at[z], z_sems.at[0, k], z_sems.at[1, k], {"dp": to * 2 + y}
+        )
+        out.start()
+        z_copies.append(out)
+
+    for copy in return_copies:
+        copy.wait()
+    start_state = s2[...].reshape(width, width)
+    from_state = carried * jnp.dot(
+        q_ref[...], start_state, preferred_element_type=jnp.float32
+    )
+    for copy in pair_copies:
+        copy.wait()
+    depth = f_ref.shape[1]
+    per_depth = depth // rows
+    total = jnp.zeros((window, width), jnp.float32)
+    for m in range(heads):
+        total = total + jnp.dot(
+            fbuf[m],
+            wbuf[m * per_depth : (m + 1) * per_depth].reshape(depth, width),
+            preferred_element_type=jnp.float32,
+        )
+    values = total.astype(jnp.bfloat16)
+    numer = from_state + jnp.dot(combined_low, values, preferred_element_type=jnp.float32)
+    hidden_ref[...] = (numer / denominator * live).astype(jnp.bfloat16)
+    state_ref[...] = kept * start_state.astype(jnp.float32) + lax.dot_general(
+        key_scaled, values, (((0,), (0,)), ((), ())), preferred_element_type=jnp.float32
+    )
+    grad = part[me] + yrecv[z].astype(jnp.float32)
+    for k, copy in enumerate(z_copies):
+        copy.wait()
+        grad = grad + zrecv[lax.rem(z + lines - k - 1, lines)].astype(jnp.float32)
+    grad_ref[...] = grad
+
+
+def in_one_kernel(
+    stream_map,
+    lengths,
+    features,
+    query_rows,
+    key_rows,
+    log_forget,
+    in_gate,
+    value_weight,
+    state,
+    norm_state,
+    cotangent,
+):
+    slots, heads = lax.axis_size("dp"), lax.axis_size("mp")
+    window, width = query_rows.shape[1:]
+    depth = features.shape[2]
+    rows = value_weight.shape[0]
+    row_part = width // slots
+    lines = slots // 2
+    low = jnp.bfloat16
+    sems = pltpu.SemaphoreType.DMA
+    vmem = pl.BlockSpec(memory_space=pltpu.VMEM)
+    smem = pl.BlockSpec(memory_space=pltpu.SMEM)
+    hidden, new_state, new_norm, grad = pl.pallas_call(
+        functools.partial(window_kernel, slots, heads),
+        out_shape=(
+            jax.ShapeDtypeStruct((window, width), low),
+            jax.ShapeDtypeStruct((width, width), jnp.float32),
+            jax.ShapeDtypeStruct((1, width), jnp.float32),
+            jax.ShapeDtypeStruct((rows, width), jnp.float32),
+        ),
+        in_specs=[smem, smem] + [vmem] * 9,
+        out_specs=(vmem, vmem, vmem, vmem),
+        scratch_shapes=[
+            pltpu.VMEM((heads, window, depth), low),
+            pltpu.VMEM((slots, rows, width), low),
+            pltpu.VMEM((slots, 1, width), jnp.float32),
+            pltpu.VMEM((slots, row_part, width), low),
+            pltpu.VMEM((slots, row_part, width), low),
+            pltpu.VMEM((slots, row_part, width), low),
+            pltpu.VMEM((slots, row_part, width), low),
+            pltpu.VMEM((slots, rows, width), jnp.float32),
+            pltpu.VMEM((slots, rows, width), low),
+            pltpu.VMEM((lines, rows, width), low),
+            pltpu.VMEM((lines, rows, width), low),
+            pltpu.VMEM((lines, rows, width), low),
+            sems((2, heads)),
+            sems((2, slots)),
+            sems((2, slots)),
+            sems((2, slots)),
+            sems((2, lines)),
+            sems((2, lines)),
+            sems((2, lines)),
+            sems((2, lines)),
+        ],
+        compiler_params=pltpu.CompilerParams(
+            collective_id=0, has_side_effects=True, vmem_limit_bytes=48 * 1024 * 1024
+        ),
+    )(
+        stream_map,
+        lengths,
+        features[0],
+        query_rows[0],
+        key_rows[0],
+        log_forget[0],
+        in_gate[0],
+        value_weight,
+        state[0, 0].reshape(slots, row_part, width),
+        norm_state[0],
+        cotangent[0],
+    )
+    return (hidden[None], new_state[None, None], new_norm[None], grad)
+
+
+def on_device(*args):
+    slots, heads = lax.axis_size("dp"), lax.axis_size("mp")
+    depth, rows, width = args[2].shape[2], args[7].shape[0], args[8].shape[-1]
+    whole_tiles = slots % 2 == 0 and width % (16 * slots) == 0 and rows % 128 == 0
+    if whole_tiles and depth % rows == 0 and depth * heads == rows * slots:
+        return in_one_kernel(*args)
+    return with_collectives(*args)
+
+
 def solution(mesh):
     return jax.shard_map(
         on_device,

time: 191 us -> 88.8 us (0.46)
  waiting for transfers between devices: 97.7 us -> 0 us
  Pallas kernels: 0 us -> 77.4 us
  blocking collectives: 47.8 us -> 0 us
  between operations: 15.2 us -> 1.41 us
  matrix products: 10.2 us -> 0 us
  starting transfers between devices: 7.52 us -> 0 us
  other arithmetic: 4.1 us -> 0 us
  local copies, waits for them, and re-layouts: 6.33 us -> 9.7 us
    reduce_scatter x1 -> x0, waiting for transfers between devices: 85.4 us -> none  [on_device(): lax.psum_scatter(lax.dot_general(feature_all, value_grad, (((0,), (0,)),...]
    pallas_call x0 -> x1, Pallas kernels: none -> 77.4 us  [in_one_kernel(): pl.pallas_call(functools.partial(window_kernel, slots, heads), out_shape=...]
    all_gather x1 -> x0, blocking collectives: 25.1 us -> none  [migrate(): norms = lax.all_gather(norm_state[0, 0], 'dp', axis=0, tiled=False)]
    all_to_all x1 -> x0, blocking collectives: 22.6 us -> none  [migrate(): lax.all_to_all(blocks, 'dp', split_axis=0, concat_axis=0, tiled=True)]
    all_to_all x1 -> x0, waiting for transfers between devices: 10.8 us -> none  [migrate(): lax.all_to_all(picked, 'dp', split_axis=0, concat_axis=0, tiled=True)]
    dot_general x7 -> x0, matrix products: 10.2 us -> none  [the longest x1 4.19 us: on_device(): lax.dot_general(feature_all, value_grad, (((0,), (0,)), ((), ())), prefer...]
    all_to_all x1 -> x0, starting transfers between devices: 7.41 us -> none  [migrate(): lax.all_to_all(picked, 'dp', split_axis=0, concat_axis=0, tiled=True)]
    unnamed x14 -> x20, local copies, waits for them, and re-layouts: 4.1 us -> 8.08 us
  transfers between devices with their start and end apart: 4 -> 0, of which waited for: 2 -> 0; matrix products, arithmetic and copies ran while one was open for 9% -> 0% of each run, Pallas kernels for 0% -> 0%
where the time goes in v2:
time: 88.8 us; the launch traced here: 88.5 us
  Pallas kernels  77.4 us (87%)
  local copies, waits for them, and re-layouts  9.7 us (11%)
  between operations  1.41 us (2%)
    pallas_call x1, Pallas kernels, in_one_kernel(): pl.pallas_call(functools.partial(window_kernel, slots, heads), out_shape=...  77.4 us
    unnamed x20, local copies, waits for them, and re-layouts  8.08 us

profile of v2, /device:TPU:10, one launch (start us, length us, event | category | flops | bytes accessed | tf_op | source)
XLA Modules:
  0.0 88.5 jit_solution(7251982307371459819)
XLA Ops:
  0.6 0.0 copy-start.1
  1.3 0.8 copy.15.forget_ref
  2.1 0.0 copy-start.6
  2.2 0.0 copy-start.7
  2.2 0.8 copy.16.gate_ref
  3.0 0.0 copy-done.1
  3.0 0.0 copy-done.6
  3.0 0.0 copy-done.7
  3.0 0.0 copy-start
  3.0 1.2 %copy-done = f32[1,1,512,512]{3,2,1,0:T(8,128)S(1)} copy-done((f32[1,1,512,512]{3,2,1,0:T(8,128)S(1)}, f32[1,1,512,512]{3,2,1,0:T(8,128)}, u32[]{:S(2)}) %copy-start) | copy-done | bytes 1048600
  4.3 0.0 copy-start.2
  4.3 0.9 %copy-done.2 = bf16[1,256,512]{2,1,0:T(8,128)(2,1)S(1)} copy-done((bf16[1,256,512]{2,1,0:T(8,128)(2,1)S(1)}, bf16[1,256,512]{2,1,0:T(8,128)(2,1)}, u32[]{:S(2)}) %copy-start.2) | copy-done | bytes 262168
  5.2 0.0 copy-start.3
  5.2 0.9 %copy-done.3 = bf16[1,256,512]{2,1,0:T(8,128)(2,1)S(1)} copy-done((bf16[1,256,512]{2,1,0:T(8,128)(2,1)S(1)}, bf16[1,256,512]{2,1,0:T(8,128)(2,1)}, u32[]{:S(2)}) %copy-start.3) | copy-done | bytes 262168
  6.2 0.0 copy-start.4
  6.2 0.9 %copy-done.4 = bf16[256,512]{1,0:T(8,128)(2,1)S(1)} copy-done((bf16[256,512]{1,0:T(8,128)(2,1)S(1)}, bf16[256,512]{1,0:T(8,128)(2,1)}, u32[]{:S(2)}) %copy-start.4) | copy-done | bytes 262168
  7.1 0.0 copy-start.5
  7.1 0.9 %copy-done.5 = bf16[1,256,512]{2,1,0:T(8,128)(2,1)S(1)} copy-done((bf16[1,256,512]{2,1,0:T(8,128)(2,1)S(1)}, bf16[1,256,512]{2,1,0:T(8,128)(2,1)}, u32[]{:S(2)}) %copy-start.5) | copy-done | bytes 262168
  8.1 77.4 %shard_map.138 = (bf16[256,512]{1,0:T(8,128)(2,1)S(1)}, f32[512,512]{1,0:T(8,128)S(1)}, f32[1,512]{1,0:T(1,128)S(1)}, f32[256,512]{1,0:T(8,128)S(1)}) custom-call(s32[8]{0:T(128)S(1)} %copy-done.7, s32[1]{0:T(128)S(6)} %copy.21.length_ref, bf16[256,512]{1,0:T(8,128)(2,1)S(1)} %bitcast.14, bf16[256,512]{1,0:T(8,128)(2,1)S(1)} %bitcast.15, ...), custom_call_target="tpu_custom_call" | custom-call | tf_op jit(solution)/shard_map/pallas_call | solution.py:405
  85.5 0.7 copy.22
  86.2 1.0 %copy.23 = f32[1,1,512,512]{3,2,1,0:T(8,128)} copy(f32[1,1,512,512]{3,2,1,0:T(8,128)S(1)} %bitcast.12) | data formatting | bytes 2097152
  87.1 0.6 copy.24
  87.7 0.8 copy.25
Async XLA Ops:
  0.6 2.4 %copy-start.1 = (bf16[1,256,512]{2,1,0:T(8,128)(2,1)S(1)}, bf16[1,256,512]{2,1,0:T(8,128)(2,1)}, u32[]{:S(2)}) copy-start(bf16[1,256,512]{2,1,0:T(8,128)(2,1)} %param.13) | copy-start | bytes 786436
  2.1 0.9 copy-start.6
  2.2 0.9 copy-start.7
  3.0 1.2 %copy-start = (f32[1,1,512,512]{3,2,1,0:T(8,128)S(1)}, f32[1,1,512,512]{3,2,1,0:T(8,128)}, u32[]{:S(2)}) copy-start(f32[1,1,512,512]{3,2,1,0:T(8,128)} %param.19) | copy-start | bytes 3145732
  4.3 0.9 %copy-start.2 = (bf16[1,256,512]{2,1,0:T(8,128)(2,1)S(1)}, bf16[1,256,512]{2,1,0:T(8,128)(2,1)}, u32[]{:S(2)}) copy-start(bf16[1,256,512]{2,1,0:T(8,128)(2,1)} %param.14) | copy-start | bytes 786436
  5.2 0.9 %copy-start.3 = (bf16[1,256,512]{2,1,0:T(8,128)(2,1)S(1)}, bf16[1,256,512]{2,1,0:T(8,128)(2,1)}, u32[]{:S(2)}) copy-start(bf16[1,256,512]{2,1,0:T(8,128)(2,1)} %param.15) | copy-start | bytes 786436
  6.2 0.9 %copy-start.4 = (bf16[256,512]{1,0:T(8,128)(2,1)S(1)}, bf16[256,512]{1,0:T(8,128)(2,1)}, u32[]{:S(2)}) copy-start(bf16[256,512]{1,0:T(8,128)(2,1)} %w_ref.1) | copy-start | bytes 786436
  7.1 0.9 %copy-start.5 = (bf16[1,256,512]{2,1,0:T(8,128)(2,1)S(1)}, bf16[1,256,512]{2,1,0:T(8,128)(2,1)}, u32[]{:S(2)}) copy-start(bf16[1,256,512]{2,1,0:T(8,128)(2,1)} %param.21) | copy-start | bytes 786436

commit v3 on v2

--- a/solution.py
+++ b/solution.py
@@ -134,18 +134,24 @@
     map_ref,
     length_ref,
     f_ref,
+    q_hbm,
+    k_hbm,
+    forget_hbm,
+    gate_hbm,
+    w_ref,
+    s_hbm,
+    n_ref,
+    cot_hbm,
+    hidden_ref,
+    state_ref,
+    norm_ref,
+    grad_ref,
     q_ref,
     k_ref,
     forget_ref,
     gate_ref,
-    w_ref,
     s_ref,
-    n_ref,
     cot_ref,
-    hidden_ref,
-    state_ref,
-    norm_ref,
-    grad_ref,
     fbuf,
     wbuf,
     nbuf,
@@ -162,8 +168,10 @@
     n_sems,
     s1_sems,
     s2_sems,
-    wz_sems,
+    up_sems,
+    down_sems,
     wy_sems,
+    local_sems,
     y_sems,
     z_sems,
 ):
@@ -179,6 +187,23 @@
 
     def line_ahead(k):
         return lax.rem(z + k, lines)
+
+    moves = (
+        (s_hbm, s_ref),
+        (q_hbm, q_ref),
+        (k_hbm, k_ref),
+        (forget_hbm, forget_ref),
+        (gate_hbm, gate_ref),
+        (cot_hbm, cot_ref),
+        (f_ref, fbuf.at[head]),
+        (w_ref, wbuf.at[me]),
+        (n_ref, nbuf.at[me]),
+    )
+    fetches = [
+        pltpu.make_async_copy(src, dst, local_sems.at[i]) for i, (src, dst) in enumerate(moves)
+    ]
+    for fetch in fetches:
+        fetch.start()
 
     barrier = pltpu.get_barrier_semaphore()
     for k in range(1, slots):
@@ -210,6 +235,7 @@
     ]
     for copy in norm_copies + feature_copies:
         copy.start()
+    fetches[0].wait()
     sblk[...] = s_ref[...].astype(jnp.bfloat16)
     spread_copies = [
         remote(
@@ -219,25 +245,52 @@
     ]
     for copy in spread_copies:
         copy.start()
-    line_copies = [
-        remote(
-            w_ref,
-            wbuf.at[me],
-            wz_sems.at[0, k],
-            wz_sems.at[1, k],
-            {"dp": line_ahead(k) * 2 + y},
-        )
-        for k in range(1, lines)
-    ]
-    pair_copies = [remote(w_ref, wbuf.at[me], wy_sems.at[0, 0], wy_sems.at[1, 0], pair)]
-    pair_copies[0].start()
-    for copy in line_copies:
-        copy.start()
-
-    nbuf[me] = n_ref[...]
-    fbuf[head] = f_ref[...]
-    wbuf[me] = w_ref[...]
+    def on_line(i):
+        return jnp.logical_and(i >= 0, i < lines)
+
+    def hop(step, sems, j):
+        slot = (z - step * j) * 2 + y
+        to = {"dp": (z + step) * 2 + y}
+        source = w_ref if j == 0 else wbuf.at[slot]
+        return remote(source, wbuf.at[slot], sems.at[0, j], sems.at[1, j], to)
+
+    def arrival(step, sems, j):
+        slot = (z - step * (j + 1)) * 2 + y
+        to = {"dp": (z - step) * 2 + y}
+        return remote(wbuf.at[slot], wbuf.at[slot], sems.at[0, j], sems.at[1, j], to)
+
+    def hand_over(line, own=False):
+        slot = line * 2 + y
+        source = w_ref if own else wbuf.at[slot]
+        return remote(source, wbuf.at[slot], wy_sems.at[0, line], wy_sems.at[1, line], pair)
+
+    directions = ((1, up_sems), (-1, down_sems))
+
+    def pass_on(j):
+        for step, sems in directions:
+
+            @pl.when(on_line(z - step * (j + 1)))
+            def _():
+                arrival(step, sems, j).wait_recv()
+                if j + 2 < lines:
+
+                    @pl.when(on_line(z + step))
+                    def _():
+                        hop(step, sems, j + 1).start()
+
+                hand_over(z - step * (j + 1)).start()
+
+    for step, sems in directions:
+
+        @pl.when(on_line(z + step))
+        def _():
+            hop(step, sems, 0).start()
+
+    hand_over(z, True).start()
+
     s1[me] = sblk[me]
+    for fetch in fetches[1:6]:
+        fetch.wait()
 
     window, width = q_ref.shape
     length = length_ref[0]
@@ -246,15 +299,15 @@
     causal = row >= column
     diagonal = row == column
     live = (lax.broadcasted_iota(jnp.int32, (window, 1), 0) < length).astype(jnp.float32)
-
-    def as_row(x):
-        return jnp.sum(jnp.where(diagonal, x, 0.0), axis=0, keepdims=True)
-
-    weights_in = jnp.exp(gate_ref[...]) * live
+    live_row = (lax.broadcasted_iota(jnp.int32, (1, window), 1) < length).astype(jnp.float32)
+
+    weights_row = jnp.exp(gate_ref[...]) * live_row
+    weights_in = jnp.sum(jnp.where(diagonal, weights_row, 0.0), axis=1, keepdims=True)
     decays = jnp.sum(
-        jnp.where(causal, as_row(forget_ref[...] * live), 0.0), axis=1, keepdims=True
-    )
-    mixing = jnp.exp(jnp.where(causal, decays - as_row(decays), -1e30)) * as_row(weights_in)
+        jnp.where(causal, forget_ref[...] * live_row, 0.0), axis=1, keepdims=True
+    )
+    decays_row = jnp.sum(jnp.where(diagonal, decays, 0.0), axis=0, keepdims=True)
+    mixing = jnp.exp(jnp.where(causal, decays - decays_row, -1e30)) * weights_row
     scale = width**-0.5
     scores = lax.dot_general(
         q_ref[...], k_ref[...], (((1,), (1,)), ((), ())), preferred_element_type=jnp.float32
@@ -274,6 +327,7 @@
             found = jnp.where(map_ref[s] == p, jnp.int32(s), found)
         return found
 
+    fetches[8].wait()
     for copy in norm_copies:
         copy.wait()
     start_norm = nbuf[source_of(me)]
@@ -287,6 +341,7 @@
         combined_low, scaled, (((0,), (0,)), ((), ())), preferred_element_type=jnp.float32
     ).astype(jnp.bfloat16)
 
+    pass_on(0)
     for copy in spread_copies:
         copy.wait()
     for p in range(slots):
@@ -301,6 +356,7 @@
         copy.start()
     s2[me] = picked[me]
 
+    fetches[6].wait()
     for copy in feature_copies:
         copy.wait()
     rows = grad_ref.shape[0]
@@ -329,12 +385,8 @@
     for copy in y_copies:
         copy.start()
 
-    for k in range(1, lines):
-        line_copies[k - 1].wait()
-        slot = lax.rem(z + lines - k, lines) * 2 + y
-        forward = remote(wbuf.at[slot], wbuf.at[slot], wy_sems.at[0, k], wy_sems.at[1, k], pair)
-        forward.start()
-        pair_copies.append(forward)
+    for j in range(1, lines - 1):
+        pass_on(j)
 
     z_copies = []
     for k, copy in zip(order, y_copies):
@@ -355,8 +407,23 @@
     from_state = carried * jnp.dot(
         q_ref[...], start_state, preferred_element_type=jnp.float32
     )
-    for copy in pair_copies:
-        copy.wait()
+    fetches[7].wait()
+    for line in range(lines):
+        handed = remote(
+            w_ref,
+            wbuf.at[line * 2 + other],
+            wy_sems.at[0, line],
+            wy_sems.at[1, line],
+            pair,
+        )
+        handed.wait()
+    for j in range(lines - 1):
+        for step, sems in directions:
+
+            @pl.when(jnp.logical_and(on_line(z + step), on_line(z - step * j)))
+            def _():
+                hop(step, sems, j).wait_send()
+
     depth = f_ref.shape[1]
     per_depth = depth // rows
     total = jnp.zeros((window, width), jnp.float32)
@@ -410,9 +477,15 @@
             jax.ShapeDtypeStruct((1, width), jnp.float32),
             jax.ShapeDtypeStruct((rows, width), jnp.float32),
         ),
-        in_specs=[smem, smem] + [vmem] * 9,
+        in_specs=[smem, smem] + [pl.BlockSpec(memory_space=pltpu.HBM)] * 9,
         out_specs=(vmem, vmem, vmem, vmem),
         scratch_shapes=[
+            pltpu.VMEM((window, width), low),
+            pltpu.VMEM((window, width), low),
+            pltpu.VMEM((1, window), jnp.float32),
+            pltpu.VMEM((1, window), jnp.float32),
+            pltpu.VMEM((slots, row_part, width), jnp.float32),
+            pltpu.VMEM((window, width), low),
             pltpu.VMEM((heads, window, depth), low),
             pltpu.VMEM((slots, rows, width), low),
             pltpu.VMEM((slots, 1, width), jnp.float32),
@@ -432,10 +505,12 @@
             sems((2, lines)),
             sems((2, lines)),
             sems((2, lines)),
+            sems((9,)),
+            sems((2, lines)),
             sems((2, lines)),
         ],
         compiler_params=pltpu.CompilerParams(
-            collective_id=0, has_side_effects=True, vmem_limit_bytes=48 * 1024 * 1024
+            collective_id=0, has_side_effects=True, vmem_limit_bytes=60 * 1024 * 1024
         ),
     )(
         stream_map,
@@ -443,8 +518,8 @@
         features[0],
         query_rows[0],
         key_rows[0],
-        log_forget[0],
-        in_gate[0],
+        log_forget.reshape(1, window),
+        in_gate.reshape(1, window),
         value_weight,
         state[0, 0].reshape(slots, row_part, width),
         norm_state[0],

time: 88.8 us -> 78.7 us (0.89)
  the two profiles are of different devices: /device:TPU:10 before, /device:TPU:0 now
where the time goes in v3:
time: 78.7 us; the launch traced here: 78.5 us
  Pallas kernels  71.8 us (91%)
  local copies, waits for them, and re-layouts  5.37 us (7%)
  between operations  1.29 us (2%)
    pallas_call x1, Pallas kernels, in_one_kernel(): pl.pallas_call(functools.partial(window_kernel, slots, heads), out_shape=...  71.8 us
    unnamed x8, local copies, waits for them, and re-layouts  5.37 us

profile of v3, /device:TPU:0, one launch (start us, length us, event | category | flops | bytes accessed | tf_op | source)
XLA Modules:
  0.0 78.5 jit_solution(15182579858643119011)
XLA Ops:
  1.3 71.8 %shard_map.138 = (bf16[256,512]{1,0:T(8,128)(2,1)}, f32[512,512]{1,0:T(8,128)}, f32[1,512]{1,0:T(1,128)}, f32[256,512]{1,0:T(8,128)}) custom-call(s32[8]{0:T(128)} %map_ref.1, s32[1]{0:T(128)S(6)} %copy.19.length_ref, bf16[256,512]{1,0:T(8,128)(2,1)} %bitcast.13, bf16[256,512]{1,0:T(8,128)(2,1)} %bitcast.14, bf16[256,512]{1,0:T(8,128)(2,1)} %bitcast.15, ...), custom_call_target="tpu_custom_call" | custom-call | tf_op jit(solution)/shard_map/pallas_call | solution.py:472
  73.1 1.7 %copy.20 = bf16[1,256,512]{2,1,0:T(8,128)(2,1)} copy(bf16[1,256,512]{2,1,0:T(8,128)(2,1)} %bitcast.17) | data formatting | bytes 524288
  74.8 0.0 copy-start.1
  74.8 0.0 copy-start
  74.8 2.3 %copy.21 = f32[1,1,512,512]{3,2,1,0:T(8,128)} copy(f32[1,1,512,512]{3,2,1,0:T(8,128)} %bitcast.12) | data formatting | bytes 2097152
  77.1 0.0 copy-done.1
  77.1 0.6 copy.22
  77.7 0.0 copy-done
  77.7 0.8 %copy.23 = f32[256,512]{1,0:T(8,128)} copy(f32[256,512]{1,0:T(8,128)S(1)} %copy-done) | data formatting | bytes 1048576
Async XLA Ops:
  74.8 2.3 %copy-start.1 = (f32[1,512]{1,0:T(1,128)S(1)}, f32[1,512]{1,0:T(1,128)}, u32[]{:S(2)}) copy-start(f32[1,512]{1,0:T(1,128)} %get-tuple-element.10) | copy-start | bytes 6148
  74.8 2.9 %copy-start = (f32[256,512]{1,0:T(8,128)S(1)}, f32[256,512]{1,0:T(8,128)}, u32[]{:S(2)}) copy-start(f32[256,512]{1,0:T(8,128)} %get-tuple-element.19) | copy-start | bytes 1572868

commit v4 on v3

--- a/solution.py
+++ b/solution.py
@@ -278,6 +278,11 @@
                     def _():
                         hop(step, sems, j + 1).start()
 
+    def hand_on(j):
+        for step, _ in directions:
+
+            @pl.when(on_line(z - step * (j + 1)))
+            def _():
                 hand_over(z - step * (j + 1)).start()
 
     for step, sems in directions:
@@ -342,6 +347,7 @@
     ).astype(jnp.bfloat16)
 
     pass_on(0)
+    hand_on(0)
     for copy in spread_copies:
         copy.wait()
     for p in range(slots):
@@ -400,6 +406,8 @@
         )
         out.start()
         z_copies.append(out)
+    for j in range(1, lines - 1):
+        hand_on(j)
 
     for copy in return_copies:
         copy.wait()

time: 78.7 us -> 84 us (1.067)
  the two profiles are of different devices: /device:TPU:0 before, /device:TPU:10 now
where the time goes in v4:
time: 84 us; the launch traced here: 83.8 us
  Pallas kernels  77.1 us (92%)
  local copies, waits for them, and re-layouts  5.37 us (6%)
  between operations  1.29 us (2%)
    pallas_call x1, Pallas kernels, in_one_kernel(): pl.pallas_call(functools.partial(window_kernel, slots, heads), out_shape=...  77.1 us
    unnamed x8, local copies, waits for them, and re-layouts  5.37 us

profile of v4, /device:TPU:10, one launch (start us, length us, event | category | flops | bytes accessed | tf_op | source)
XLA Modules:
  0.0 83.8 jit_solution(13815542598705169158)
XLA Ops:
  1.3 77.1 %shard_map.138 = (bf16[256,512]{1,0:T(8,128)(2,1)}, f32[512,512]{1,0:T(8,128)}, f32[1,512]{1,0:T(1,128)}, f32[256,512]{1,0:T(8,128)}) custom-call(s32[8]{0:T(128)} %map_ref.1, s32[1]{0:T(128)S(6)} %copy.19.length_ref, bf16[256,512]{1,0:T(8,128)(2,1)} %bitcast.13, bf16[256,512]{1,0:T(8,128)(2,1)} %bitcast.14, bf16[256,512]{1,0:T(8,128)(2,1)} %bitcast.15, ...), custom_call_target="tpu_custom_call" | custom-call | tf_op jit(solution)/shard_map/pallas_call | solution.py:480
  78.4 1.7 %copy.20 = bf16[1,256,512]{2,1,0:T(8,128)(2,1)} copy(bf16[1,256,512]{2,1,0:T(8,128)(2,1)} %bitcast.17) | data formatting | bytes 524288
  80.1 0.0 copy-start.1
  80.1 0.0 copy-start
  80.1 2.3 %copy.21 = f32[1,1,512,512]{3,2,1,0:T(8,128)} copy(f32[1,1,512,512]{3,2,1,0:T(8,128)} %bitcast.12) | data formatting | bytes 2097152
  82.4 0.0 copy-done.1
  82.4 0.6 copy.22
  83.0 0.0 copy-done
  83.0 0.8 copy.23
Async XLA Ops:
  80.1 2.3 %copy-start.1 = (f32[1,512]{1,0:T(1,128)S(1)}, f32[1,512]{1,0:T(1,128)}, u32[]{:S(2)}) copy-start(f32[1,512]{1,0:T(1,128)} %get-tuple-element.10) | copy-start | bytes 6148
  80.1 2.9 %copy-start = (f32[256,512]{1,0:T(8,128)S(1)}, f32[256,512]{1,0:T(8,128)}, u32[]{:S(2)}) copy-start(f32[256,512]{1,0:T(8,128)} %get-tuple-element.19) | copy-start | bytes 1572868

commit v5 on v3

--- a/solution.py
+++ b/solution.py
@@ -361,6 +361,16 @@
         copy.wait()
     rows = grad_ref.shape[0]
     per_head = f_ref.shape[1] // rows
+
+    def exchange(line):
+        return remote(
+            psend.at[line * 2 + other],
+            yrecv.at[line],
+            y_sems.at[0, line],
+            y_sems.at[1, line],
+            pair,
+        )
+
     for r in range(slots):
         lower = (r % per_head) * rows
         block = lax.dot_general(
@@ -371,35 +381,25 @@
         )
         part[r] = block
         psend[r] = block.astype(jnp.bfloat16)
-    order = list(range(1, lines)) + [0]
-    y_copies = [
-        remote(
-            psend.at[line_ahead(k) * 2 + other],
-            yrecv.at[line_ahead(k)],
-            y_sems.at[0, k],
-            y_sems.at[1, k],
-            pair,
-        )
-        for k in order
-    ]
-    for copy in y_copies:
-        copy.start()
-
-    for j in range(1, lines - 1):
-        pass_on(j)
-
+
+        @pl.when(other == r % 2)
+        def _():
+            exchange(r // 2).start()
+
+    pass_on(1)
     z_copies = []
-    for k, copy in zip(order, y_copies):
-        copy.wait()
-        if k == 0:
-            continue
+    for k in range(1, lines):
         to = line_ahead(k)
+        exchange(to).wait()
         zsend[to] = (part[to * 2 + y] + yrecv[to].astype(jnp.float32)).astype(jnp.bfloat16)
         out = remote(
             zsend.at[to], zrecv.at[z], z_sems.at[0, k], z_sems.at[1, k], {"dp": to * 2 + y}
         )
         out.start()
         z_copies.append(out)
+        if 1 < k + 1 < lines - 1:
+            pass_on(k + 1)
+    exchange(z).wait()
 
     for copy in return_copies:
         copy.wait()

time: 78.7 us -> 85.6 us (1.088)
  the two profiles are of different devices: /device:TPU:0 before, /device:TPU:10 now
where the time goes in v5:
time: 85.6 us; the launch traced here: 84.4 us
  Pallas kernels  77.7 us (91%)
  local copies, waits for them, and re-layouts  5.37 us (6%)
  between operations  1.29 us (2%)
    pallas_call x1, Pallas kernels, in_one_kernel(): pl.pallas_call(functools.partial(window_kernel, slots, heads), out_shape=...  77.7 us
    unnamed x8, local copies, waits for them, and re-layouts  5.37 us

profile of v5, /device:TPU:10, one launch (start us, length us, event | category | flops | bytes accessed | tf_op | source)
XLA Modules:
  0.0 84.4 jit_solution(6389662463937118800)
XLA Ops:
  1.3 77.7 %shard_map.138 = (bf16[256,512]{1,0:T(8,128)(2,1)}, f32[512,512]{1,0:T(8,128)}, f32[1,512]{1,0:T(1,128)}, f32[256,512]{1,0:T(8,128)}) custom-call(s32[8]{0:T(128)} %map_ref.1, s32[1]{0:T(128)S(6)} %copy.19.length_ref, bf16[256,512]{1,0:T(8,128)(2,1)} %bitcast.13, bf16[256,512]{1,0:T(8,128)(2,1)} %bitcast.14, bf16[256,512]{1,0:T(8,128)(2,1)} %bitcast.15, ...), custom_call_target="tpu_custom_call" | custom-call | tf_op jit(solution)/shard_map/pallas_call | solution.py:472
  79.0 1.7 %copy.20 = bf16[1,256,512]{2,1,0:T(8,128)(2,1)} copy(bf16[1,256,512]{2,1,0:T(8,128)(2,1)} %bitcast.17) | data formatting | bytes 524288
  80.7 0.0 copy-start.1
  80.7 0.0 copy-start
  80.7 2.3 %copy.21 = f32[1,1,512,512]{3,2,1,0:T(8,128)} copy(f32[1,1,512,512]{3,2,1,0:T(8,128)} %bitcast.12) | data formatting | bytes 2097152
  83.0 0.0 copy-done.1
  83.0 0.6 copy.22
  83.6 0.0 copy-done
  83.6 0.8 copy.23
Async XLA Ops:
  80.7 2.3 %copy-start.1 = (f32[1,512]{1,0:T(1,128)S(1)}, f32[1,512]{1,0:T(1,128)}, u32[]{:S(2)}) copy-start(f32[1,512]{1,0:T(1,128)} %get-tuple-element.10) | copy-start | bytes 6148
  80.7 2.9 %copy-start = (f32[256,512]{1,0:T(8,128)S(1)}, f32[256,512]{1,0:T(8,128)}, u32[]{:S(2)}) copy-start(f32[256,512]{1,0:T(8,128)} %get-tuple-element.19) | copy-start | bytes 1572868
